TPU v7x, 32 devices: a whole 2x2x4 slice. The times are simulated.
32 devices in a mesh: groups: 2 (over y), traj: 16 (over z, x, core).
Axes of the slice: x: 2, y: 2, z: 4, core: 2. Of those that a mesh axis runs over, the one named last changes fastest.
Arguments:
- trajectories: bfloat16 [16384, 192], P(('groups', 'traj')), parts along dimension 0
- landmark_index: int32 [1024], P(('groups', 'traj')), parts along dimension 0, may hold values from 0 to 8191, as said below
- start_vectors: float32 [16384, 32], P(('groups', 'traj')), parts along dimension 0, may hold values from -6 to 6
Outputs:
- embedding: float32 [16384, 32], P(('groups', 'traj')), parts along dimension 0
There are 2 independent parts, one for each index of `groups`. A program takes and returns all parts, laid end to end along the dimension named above; each array names one. Nothing has to cross between parts.
Inputs may be any that keep to these rules, and one draw needn't show every extreme that they name: `landmark_index`: entries b * 32 to (b + 1) * 32 - 1 are distinct rows of the range b * 512 to (b + 1) * 512 - 1, for every b.
All inputs are finite; a program needn't handle non-finite values.
Results may differ from a plain program's by a relative error of at most 0.0003.
Values may be sent and summed in bfloat16 or wider, within the bound.
A program may use at most 64 MiB of HBM per device.

v0:
```python
import math

import jax
import jax.numpy as jnp
from jax import lax
from jax.sharding import PartitionSpec as P

SWEEPS = 2


HIGH = lax.Precision.HIGHEST


def kernel_turned(rows, row_norms, lands):
    wide = lands.astype(jnp.float32)
    land_norms = jnp.sum(wide * wide, axis=1)
    cross = lax.dot_general(
        lands, rows, (((1,), (1,)), ((), ())), preferred_element_type=jnp.float32
    )
    dist = land_norms[:, None] + row_norms[None, :] - 2.0 * cross
    return jnp.exp(-dist * (2.0 / rows.shape[1]))


def column_fold(rows, row_norms, weighted):

    def fold(total, piece, start):
        count = piece.shape[0]
        width = math.gcd(count, 512)

        def step_block(j, acc):
            lands = lax.dynamic_slice_in_dim(piece, j * width, width, 0)
            block = kernel_turned(rows, row_norms, lands)
            part = jnp.dot(block, weighted, precision=HIGH, preferred_element_type=jnp.float32)
            return lax.dynamic_update_slice_in_dim(acc, part, j * width, 0)

        return lax.fori_loop(0, count // width, step_block, total)

    return fold


def row_fold(rows, row_norms, mixing):

    def fold(total, piece, start):
        count = piece.shape[0]
        width = math.gcd(count, 512)

        def step_block(j, acc):
            lands = lax.dynamic_slice_in_dim(piece, j * width, width, 0)
            block = kernel_turned(rows, row_norms, lands)
            mix = lax.dynamic_slice_in_dim(mixing, j * width, width, 0)
            return acc + lax.dot_general(
                block,
                mix,
                (((0,), (0,)), ((), ())),
                precision=HIGH,
                preferred_element_type=jnp.float32,
            )

        return lax.fori_loop(0, count // width, step_block, total)

    return fold


def over_columns(rows, row_norms, weighted, own_lands):
    total_lands = own_lands.shape[0] * lax.axis_size("traj")
    start = jnp.zeros((total_lands, weighted.shape[1]), jnp.float32)
    fold = column_fold(rows, row_norms, weighted)
    return fold(start, lax.all_gather(own_lands, "traj", axis=0, tiled=True), jnp.int32(0))


def over_rows(rows, row_norms, mixing, own_lands):
    start = jnp.zeros((rows.shape[0], mixing.shape[1]), jnp.float32)
    fold = row_fold(rows, row_norms, mixing)
    return fold(start, lax.all_gather(own_lands, "traj", axis=0, tiled=True), jnp.int32(0))


def orthonormal(block, gram):
    lower = jnp.linalg.cholesky(gram)
    return jax.scipy.linalg.solve_triangular(lower, block.T, lower=True).T


def orthonormal_upper(block, gram):
    return orthonormal(block[:, ::-1], gram[::-1, ::-1])[:, ::-1]


def landmark_reduce(partial_value, scale_all):
    total = lax.psum(partial_value, "traj")
    return total / scale_all


def local(trajectories, landmark_index, start_vectors):
    row_dev = trajectories.shape[0]
    wide_rows = trajectories.astype(jnp.float32)
    row_norms = jnp.sum(wide_rows * wide_rows, axis=1)
    local_index = landmark_index - lax.axis_index("traj") * row_dev
    own_lands = jnp.take(trajectories, local_index, axis=0)
    own_norms = jnp.take(row_norms, local_index, axis=0)
    total_lands = own_lands.shape[0] * lax.axis_size("traj")
    land_deg = over_rows(own_lands, own_norms, jnp.ones((total_lands, 1), jnp.float32), own_lands)
    deg_all = lax.all_gather(land_deg, "traj", axis=0, tiled=True)
    col_part = over_columns(trajectories, row_norms, jnp.ones((row_dev, 1), jnp.float32), own_lands)
    ratio = landmark_reduce(col_part, deg_all)
    degree = over_rows(trajectories, row_norms, ratio, own_lands)
    dinv = lax.rsqrt(degree)
    vectors = start_vectors
    gram_part = None
    for sweep in range(SWEEPS):
        if gram_part is not None:
            gram = lax.psum(gram_part, "traj")
            vectors = orthonormal_upper(vectors, gram)
        partial_value = over_columns(trajectories, row_norms, dinv * vectors, own_lands)
        scaled = landmark_reduce(partial_value, deg_all)
        vectors = dinv * over_rows(trajectories, row_norms, scaled, own_lands)
        gram_part = jnp.dot(vectors.T, vectors, precision=HIGH, preferred_element_type=jnp.float32)
    gram = lax.psum(gram_part, "traj")
    vectors = orthonormal(vectors, gram)
    return math.sqrt(row_dev * lax.axis_size("traj")) * vectors


def solution(mesh):
    return jax.shard_map(
        local,
        mesh=mesh,
        in_specs=(P(("groups", "traj"), None), P(("groups", "traj")), P(("groups", "traj"), None)),
        out_specs=P(("groups", "traj"), None),
        check_vma=False,
    )
```

profile of v0, /device:TPU:0, one launch (start us, length us, event | category | flops | bytes accessed | tf_op | source)
XLA Modules:
  0.0 389.3 jit_solution(15879041102556417802)
XLA Ops:
  6.5 0.0 copy-start
  6.5 0.0 all-reduce.5.cloned.1.call-start
  6.5 1.1 multiply_reduce_fusion.1
  7.6 0.0 copy-done
  7.6 0.1 copy.9
  7.7 0.0 copy-start.2
  7.8 0.6 copy-done.2
  8.4 0.7 gather_fusion.1
  9.1 0.6 gather_fusion
  9.8 0.1 broadcast_select_fusion
  9.8 23.8 %all_gather.4 = bf16[512,192]{1,0:T(8,128)(2,1)S(1)} all-gather(bf16[32,192]{1,0:T(8,128)(2,1)S(1)} %broadcast_select_fusion), channel_id=1, replica_groups=mesh['groups'=2,'traj'=16] {'traj'}, dimensions={0}, use_global_device_ids=true | all-gather | bytes 208896 | tf_op jit(solution)/shard_map/all_gather | solution.py:74
  33.6 0.1 multiply_reduce_fusion
  33.8 0.4 fusion.3
  34.1 0.2 fusion.7
  34.4 0.3 convolution_bitcast_fusion.2
  34.6 0.0 copy-start.3
  34.6 1.0 convolution_bitcast_fusion.1
  35.6 0.0 copy-done.3
  35.6 0.6 dynamic-slice
  36.9 0.2 dynamic-update-slice.2
  37.1 29.8 %all-reduce.1 = (f32[512,1]{0,1:T(1,128)S(1)}, f32[512]{0:T(512)S(1)}) all-reduce(f32[512,1]{0,1:T(1,128)S(1)} %convolution_bitcast_fusion.1, f32[512]{0:T(512)S(1)} %dynamic-update-slice.2), channel_id=1, replica_groups=mesh['groups'=2,'traj'=16] {'traj'}, use_global_device_ids=true, to_apply=%region_2.3 | all-reduce | flops 1024 | bytes 8192 | tf_op jit(solution)/shard_map/psum | solution.py:87
  66.9 0.0 copy-start.1
  66.9 0.7 fusion.29
  67.6 0.2 copy-done.1
  67.8 1.7 fusion.17
  69.4 0.0 all-reduce.5.cloned.1.call-update
  69.5 0.0 all-reduce.7.cloned.1.call-start
  69.5 86.2 %all-reduce.5.cloned.1.call-done = f32[512,32]{1,0:T(8,128)} async-done(((f32[512,32]{1,0:T(8,128)}), f32[512,32]{1,0:T(8,128)}) %all-reduce.5.cloned.1.call-update) | async-done | bytes 65552 | tf_op jit(solution)/shard_map/psum | solution.py:87
  155.7 1.7 convolution_multiply_fusion.4
  157.4 0.2 fusion.35
  157.7 0.1 rev.10
  157.8 0.1 rev.9
  157.8 60.0 %psum.37 = f32[32,32]{0,1:T(8,128)S(1)} all-reduce(f32[32,32]{0,1:T(8,128)S(1)} %rev.9), channel_id=1, replica_groups=mesh['groups'=2,'traj'=16] {'traj'}, use_global_device_ids=true, to_apply=%region_4.5 | all-reduce | flops 1024 | bytes 8192 | tf_op jit(solution)/shard_map/psum | solution.py:109
  217.8 0.1 copy.11
  217.9 2.9 cholesky.44
  220.9 0.6 compare_reduce_fusion.1
  221.5 0.7 fusion.21
  222.2 2.5 custom-call.6
  224.6 0.3 convolution_bitcast_fusion
  224.9 0.1 rev.11
  225.0 1.7 fusion.15
  226.7 0.0 all-reduce.7.cloned.1.call-update
  226.7 86.2 %all-reduce.7.cloned.1.call-done = f32[512,32]{1,0:T(8,128)} async-done(((f32[512,32]{1,0:T(8,128)}), f32[512,32]{1,0:T(8,128)}) %all-reduce.7.cloned.1.call-update) | async-done | bytes 65552 | tf_op jit(solution)/shard_map/psum | solution.py:87
  312.9 1.7 convolution_multiply_fusion.3
  314.6 0.2 fusion.36
  314.8 60.0 %psum.39 = f32[32,32]{0,1:T(8,128)S(1)} all-reduce(f32[32,32]{0,1:T(8,128)S(1)} %fusion.36), channel_id=1, replica_groups=mesh['groups'=2,'traj'=16] {'traj'}, use_global_device_ids=true, to_apply=%region_8.11 | all-reduce | flops 1024 | bytes 8192 | tf_op jit(solution)/shard_map/psum | solution.py:115
  374.8 0.1 copy.13
  374.9 2.9 cholesky.55
  377.8 0.6 compare_reduce_fusion
  378.5 0.7 fusion.22
  379.1 2.4 custom-call.7
  381.6 0.9 fusion.8
  (9 shorter events, 0.1 us)
Async XLA Ops:
  6.5 1.1 copy-start
  6.5 149.2 %all-reduce.5.cloned.1.call-start = ((), (), s32[]{:S(2)}) async-start(), calls=%async_computation | async-start | bytes 524288 | tf_op jit(solution)/shard_map/psum | solution.py:87
  7.7 0.7 copy-start.2
  34.6 1.0 copy-start.3
  66.9 0.8 copy-start.1
  69.5 243.4 %all-reduce.7.cloned.1.call-start = ((), (), s32[]{:S(2)}) async-start(), calls=%async_computation.1 | async-start | bytes 524288 | tf_op jit(solution)/shard_map/psum | solution.py:87
Sparse Core Ops, SparseCore 0:
  69.6 86.0 all-reduce.4
  226.8 85.9 all-reduce.6
where the time goes:
time: 390 us; the launch traced here: 389 us
  blocking collectives  174 us (45%)
  waiting for transfers between devices  172 us (44%)
  other arithmetic  14.7 us (4%)
  between operations  14.2 us (4%)
  matrix products  10.9 us (3%)
    psum x2, waiting for transfers between devices, landmark_reduce(): total = lax.psum(partial_value, 'traj')  172 us
    psum x2, blocking collectives, local(): gram = lax.psum(gram_part, 'traj')  120 us
    psum x1, blocking collectives, landmark_reduce(): total = lax.psum(partial_value, 'traj')  29.8 us
    all_gather x1, blocking collectives, over_rows(): lax.all_gather(own_lands, 'traj', axis=0, tiled=True)  23.8 us
  transfers between devices with their start and end apart: 2, of which 2 were waited for; matrix products, arithmetic and copies ran while one was open for 0% of the time, Pallas kernels for 0%

commit v1 on v0

v1 whole, which is shorter than its diff:
```python
import functools
import math

import jax
import jax.numpy as jnp
from jax import lax
from jax.experimental import pallas as pl
from jax.experimental.pallas import tpu as pltpu
from jax.sharding import PartitionSpec as P

F32 = jnp.float32
BF16 = jnp.bfloat16
HIGH = lax.Precision.HIGHEST
MESH = pl.DeviceIdType.MESH
VECS = 32
OWN = 32
HALF = OWN // 2
NT = (((1,), (1,)), ((), ()))
NN = (((1,), (0,)), ((), ()))


def mxu(a, b, dims=NN):
    return lax.dot_general(a, b, dims, preferred_element_type=F32)


def exact(a, b, dims=NN):
    return lax.dot_general(a, b, dims, precision=HIGH, preferred_element_type=F32)


def split2(x):
    hi = x.astype(BF16)
    lo = (x - hi.astype(F32)).astype(BF16)
    return jnp.concatenate([hi, lo], axis=0)


def inverse_factor(gram, reverse):
    lane = lax.broadcasted_iota(jnp.int32, (8, 128), 1)
    sub = lax.broadcasted_iota(jnp.int32, (8, 128), 0)
    nblk = VECS // 8
    blocks = []
    for a in range(nblk):
        unit = (lane == sub + (VECS + 8 * a)).astype(F32)
        blocks.append(jnp.where(lane < VECS, gram[8 * a : 8 * a + 8, :], unit))
    order = range(VECS - 1, -1, -1) if reverse else range(VECS)
    for j in order:
        a, s = divmod(j, 8)
        pivot = blocks[a][s : s + 1, :]
        scaled = pivot * (1.0 / pivot[:, j : j + 1])
        for c in range(nblk):
            if (c > a and not reverse) or (c < a and reverse):
                blocks[c] = blocks[c] - blocks[c][:, j : j + 1] * scaled
            elif c == a:
                keep = sub < s if reverse else sub > s
                blocks[c] = blocks[c] - jnp.where(keep, blocks[c][:, j : j + 1], 0.0) * scaled
    done = []
    for a in range(nblk):
        diag = jnp.sum(jnp.where(lane == sub + 8 * a, blocks[a], 0.0), axis=1, keepdims=True)
        done.append(blocks[a] * lax.rsqrt(diag))
    whole = jnp.concatenate(done, axis=0)
    return whole[:, VECS : 2 * VECS]


def body(n, total_rows, xt_ref, idx_ref, qt_ref, out_ref,
         lsrc, lbuf, x_a, x_b, cmat, own_c, chi, clo, csrc, cbuf,
         z1, r1, t1, a1, z2, r2, t2, a2, gsrc, gbuf, send, recv):
    me = lax.axis_index("traj")
    rows = xt_ref.shape[1]
    feat = xt_ref.shape[0]
    rest = feat - 128
    lands = OWN * n
    side = HALF * n
    lt = lands // 128
    scale = 2.0 / feat

    def peer(d):
        return lax.rem(me + d, n)

    def spread(k, source, target):
        @pl.loop(1, n)
        def _(d):
            to = peer(d)
            pltpu.make_async_remote_copy(
                src_ref=source(to), dst_ref=target.at[me],
                send_sem=send.at[k], recv_sem=recv.at[k],
                device_id={"traj": to}, device_id_type=MESH,
            ).start()

    def arrived(k, target):
        part = target.at[pl.ds(0, n - 1)]
        pltpu.make_async_copy(part, part, recv.at[k]).wait()

    def left(k, target):
        part = target.at[pl.ds(0, n - 1)]
        pltpu.make_async_copy(part, part, send.at[k]).wait()

    barrier = pltpu.get_barrier_semaphore()

    @pl.loop(1, n)
    def _(d):
        pl.semaphore_signal(barrier, inc=1, device_id={"traj": peer(d)}, device_id_type=MESH)

    xt = xt_ref[...]
    gap = jnp.zeros((256 - feat, rows), BF16)
    xt_a = jnp.concatenate([xt, gap], axis=0)
    xt_b = jnp.concatenate([xt[:128], gap, xt[128:]], axis=0)
    idx = idx_ref[...] - me * rows
    eye = lax.broadcasted_iota(jnp.int32, (OWN, OWN), 0) == lax.broadcasted_iota(jnp.int32, (OWN, OWN), 1)
    idx_col = jnp.sum(jnp.where(eye, jnp.broadcast_to(idx, (OWN, OWN)).astype(F32), 0.0), axis=1, keepdims=True)
    spot = lax.broadcasted_iota(jnp.int32, (OWN, rows), 1).astype(F32)
    hot = (spot == idx_col).astype(F32).astype(BF16)
    own_a = mxu(hot, xt_a, NT)
    own_b = mxu(hot, xt_b, NT)
    lsrc[0] = own_a[:HALF, :128].astype(BF16)
    lsrc[1] = own_a[HALF:, :128].astype(BF16)
    lsrc[2] = (own_a[:HALF, 128:] + own_b[HALF:, 128:]).astype(BF16)

    pl.semaphore_wait(barrier, n - 1)
    spread(0, lambda to: lsrc, lbuf)
    lbuf[me] = lsrc[...]

    x_a[:rows] = jnp.transpose(xt_a)
    x_b[:rows] = jnp.transpose(xt_b)
    x_a[rows:] = own_a.astype(BF16)
    x_b[rows:] = own_b.astype(BF16)
    wide = x_a[...].astype(F32)
    row_norms = jnp.sum(wide * wide, axis=1, keepdims=True) * scale
    lane256 = lax.broadcasted_iota(jnp.int32, (16, 256), 1)
    mask_a = (lane256 < feat).astype(F32).astype(BF16)
    mask_b = ((lane256 < 128) | (lane256 >= 256 - rest)).astype(F32).astype(BF16)

    arrived(0, lbuf)
    width = min(side, 256)
    own_sum = jnp.zeros((OWN, 1), F32)
    for half, (x, mask) in enumerate(((x_a, mask_a), (x_b, mask_b))):
        for piece in range(side // width):
            blk = pl.ds(piece * (width // HALF), width // HALF)
            land = jnp.concatenate(
                [lbuf[blk, half].reshape(width, 128), lbuf[blk, 2].reshape(width, 128)], axis=1)
            lw = land.astype(F32)
            sq = lw * lw
            sq_hi = sq.astype(BF16)
            sq_lo = (sq - sq_hi.astype(F32)).astype(BF16)
            norm = (mxu(mask, sq_hi, NT) + mxu(mask, sq_lo, NT))[0:1] * scale
            cross = mxu(x[...], land, NT)
            block = jnp.exp(cross * (2.0 * scale) - (row_norms + norm))
            at = half * side + piece * width
            cmat[:, at : at + width] = block[:rows]
            sums = jnp.sum(block[:rows], axis=0, keepdims=True)
            for b in range(width // 128):
                csrc[at // 128 + b : at // 128 + b + 1, :] = sums[:, 128 * b : 128 * b + 128]
            own_sum = own_sum + jnp.sum(block[rows:], axis=1, keepdims=True)
    lane = lax.broadcasted_iota(jnp.int32, (OWN, 128), 1)
    sub = lax.broadcasted_iota(jnp.int32, (OWN, 128), 0)
    fit = (lane // HALF == lax.rem(me, 8)) & (lax.rem(lane, HALF) == lax.rem(sub, HALF))
    placed = jnp.where(fit, own_sum, 0.0)
    place_a = jnp.sum(placed[:HALF], axis=0, keepdims=True)
    place_b = jnp.sum(placed[HALF:], axis=0, keepdims=True)
    at_row = lax.broadcasted_iota(jnp.int32, (lt // 2, 128), 0) == me // 8
    csrc[lt : lt + lt // 2] = jnp.where(at_row, place_a, 0.0)
    csrc[lt + lt // 2 : 2 * lt] = jnp.where(at_row, place_b, 0.0)
    spread(1, lambda to: csrc, cbuf)
    cbuf[me] = csrc[...]

    for at in range(0, lands, 256):
        c = cmat[:, at : at + 256]
        hi = c.astype(BF16)
        chi[:, at : at + 256] = hi
        clo[:, at : at + 256] = (c - hi.astype(F32)).astype(BF16)

    def across_rows(left_rows):
        m = left_rows.shape[0]
        s = split2(left_rows)
        r = mxu(s, chi[...]) + mxu(s, clo[...])
        return r[:m] + r[m:]

    def across_lands(left_lands):
        m = left_lands.shape[0]
        s = split2(left_lands)
        r = mxu(s, chi[...], NT) + mxu(s, clo[...], NT)
        return r[:m] + r[m:]

    def as_row(x):
        return jnp.concatenate([x[b : b + 1, :] for b in range(lt)], axis=1)

    arrived(1, cbuf)
    sums = jnp.sum(cbuf[...], axis=0)
    inv = 1.0 / sums[lt:]
    inv_row = as_row(inv)
    ratio = as_row(sums[:lt] * inv)
    degree = across_lands(jnp.broadcast_to(ratio, (8, lands)))[0:1]
    dinv = lax.rsqrt(degree)

    def reduced(k, value, zs, rs, ts, gather):
        for a in range(VECS // 8):
            for b in range(lt):
                zs[a * lt + b] = value[8 * a : 8 * a + 8, 128 * b : 128 * b + 128]
        spread(k, lambda to: zs.at[to], rs)
        rs[me] = zs[me]
        arrived(k, rs)
        ts[...] = jnp.sum(rs[...], axis=0)
        spread(k + 1, lambda to: ts, gather)
        gather[me] = ts[...]
        arrived(k + 1, gather)
        return jnp.concatenate(
            [jnp.concatenate([gather[a * lt + b] for b in range(lt)], axis=1) for a in range(VECS // 8)], axis=0)

    sums1 = reduced(2, across_rows(qt_ref[...] * dinv), z1, r1, t1, a1)
    u1 = sums1 * inv_row
    y1 = across_lands(u1) * dinv
    sums2 = reduced(4, across_rows(y1 * dinv), z2, r2, t2, a2)
    gram1 = exact(u1, jnp.concatenate([sums2] * 4, axis=0), NT)
    back = inverse_factor(gram1, True)
    y2 = exact(back, across_lands(sums2 * inv_row) * dinv)
    gram2 = exact(y2, jnp.concatenate([y2] * 4, axis=0), NT)
    packed = jnp.zeros((8, 128), F32)
    lane8 = lax.broadcasted_iota(jnp.int32, (8, 128), 1)
    for a in range(VECS // 8):
        packed = packed + jnp.where(lane8 // VECS == a, gram2[8 * a : 8 * a + 8], 0.0)
    gsrc[...] = packed
    spread(6, lambda to: gsrc, gbuf)
    gbuf[me] = gsrc[...]
    arrived(6, gbuf)
    total = jnp.sum(gbuf[...], axis=0)
    gram2 = jnp.concatenate(
        [total if a == 0 else pltpu.roll(total, 128 - VECS * a, 1) for a in range(VECS // 8)], axis=0)
    last = inverse_factor(gram2, False) * math.sqrt(total_rows)
    out_ref[...] = exact(last, y2)
    for k, buf in enumerate((lbuf, cbuf, r1, a1, r2, a2, gbuf)):
        left(k, buf)


def local(trajectories, landmark_index, start_vectors):
    n = lax.axis_size("traj")
    rows, feat = trajectories.shape
    lands = OWN * n
    lt = lands // 128
    vmem = pl.BlockSpec(memory_space=pltpu.VMEM)
    tiles = pltpu.VMEM((n, 8, 128), F32)
    tile = pltpu.VMEM((8, 128), F32)
    out = pl.pallas_call(
        functools.partial(body, n, rows * n),
        out_shape=jax.ShapeDtypeStruct((VECS, rows), F32),
        in_specs=[vmem] * 3,
        out_specs=vmem,
        scratch_shapes=[
            pltpu.VMEM((3, HALF, 128), BF16),
            pltpu.VMEM((n, 3, HALF, 128), BF16),
            pltpu.VMEM((rows + OWN, 256), BF16),
            pltpu.VMEM((rows + OWN, 256), BF16),
            pltpu.VMEM((rows, lands), F32),
            tile,
            pltpu.VMEM((rows, lands), BF16),
            pltpu.VMEM((rows, lands), BF16),
            pltpu.VMEM((2 * lt, 128), F32),
            pltpu.VMEM((n, 2 * lt, 128), F32),
            tiles, tiles, tile, tiles,
            tiles, tiles, tile, tiles,
            tile, tiles,
            pltpu.SemaphoreType.DMA((7,)),
            pltpu.SemaphoreType.DMA((7,)),
        ],
        compiler_params=pltpu.CompilerParams(
            collective_id=0, has_side_effects=True, vmem_limit_bytes=48 * 1024 * 1024),
        cost_estimate=pl.CostEstimate(flops=10**9, bytes_accessed=10**6, transcendentals=10**6),
    )(trajectories.T, landmark_index.reshape(1, OWN), start_vectors.T)
    return out.T


def solution(mesh):
    return jax.shard_map(
        local,
        mesh=mesh,
        in_specs=(P(("groups", "traj"), None), P(("groups", "traj")), P(("groups", "traj"), None)),
        out_specs=P(("groups", "traj"), None),
        check_vma=False,
    )
```

time: 390 us -> 48.7 us (0.12)
  blocking collectives: 174 us -> 0 us
  waiting for transfers between devices: 172 us -> 0 us
  Pallas kernels: 0 us -> 45.4 us
  other arithmetic: 14.7 us -> 0 us
  between operations: 14.2 us -> 0.01 us
  matrix products: 10.9 us -> 0 us
    psum x2 -> x0, waiting for transfers between devices: 172 us -> none  [landmark_reduce(): total = lax.psum(partial_value, 'traj')]
    psum x3 -> x0, blocking collectives: 150 us -> none  [the longest x2 120 us: local(): gram = lax.psum(gram_part, 'traj')]
    pallas_call x0 -> x1, Pallas kernels: none -> 45.4 us  [local(): pl.pallas_call(functools.partial(body, n, rows * n), out_shape=jax.ShapeD...]
    all_gather x1 -> x0, blocking collectives: 23.8 us -> none  [over_rows(): lax.all_gather(own_lands, 'traj', axis=0, tiled=True)]
    another operation x10 -> x0, other arithmetic: 13.4 us -> none  [the longest x6 7.19 us: orthonormal(): lower = jnp.linalg.cholesky(gram)]
    dot_general x11 -> x0, matrix products: 9.7 us -> none  [the longest x4 4.4 us: step_block(): lax.dot_general(block, mix, (((0,), (0,)), ((), ())), precision=HIGH, pre...]
  transfers between devices with their start and end apart: 2 -> 0, of which waited for: 2 -> 0; matrix products, arithmetic and copies ran while one was open for 0% -> 0% of each run, Pallas kernels for 0% -> 0%
where the time goes in v1:
time: 48.7 us; the launch traced here: 48.5 us
  Pallas kernels  45.4 us (93%)
  local copies, waits for them, and re-layouts  3.05 us (6%)
    pallas_call x1, Pallas kernels, local(): pl.pallas_call(functools.partial(body, n, rows * n), out_shape=jax.ShapeD...  45.4 us
    unnamed x7, local copies, waits for them, and re-layouts  3.05 us

profile of v1, /device:TPU:0, one launch (start us, length us, event | category | flops | bytes accessed | tf_op | source)
XLA Modules:
  0.0 48.5 jit_solution(9954478982566062248)
XLA Ops:
  0.0 0.0 copy-start.2
  0.0 0.7 %copy-done.2 = s32[32]{0:T(128)S(1)} copy-done((s32[32]{0:T(128)S(1)}, s32[32]{0:T(128)}, u32[]{:S(2)}) %copy-start.2) | copy-done | bytes 152
  0.7 0.0 copy-start
  0.7 0.9 %copy-done = bf16[512,192]{0,1:T(8,128)(2,1)S(1)} copy-done((bf16[512,192]{0,1:T(8,128)(2,1)S(1)}, bf16[512,192]{0,1:T(8,128)(2,1)}, u32[]{:S(2)}) %copy-start) | copy-done | bytes 196632
  1.6 0.0 copy-start.1
  1.6 0.8 %copy-done.1 = f32[512,32]{0,1:T(8,128)S(1)} copy-done((f32[512,32]{0,1:T(8,128)S(1)}, f32[512,32]{0,1:T(8,128)}, u32[]{:S(2)}) %copy-start.1) | copy-done | bytes 65560
  2.4 45.4 %shard_map.37 = f32[32,512]{1,0:T(8,128)S(1)} custom-call(bf16[192,512]{1,0:T(8,128)(2,1)S(1)} %bitcast.5, s32[1,32]{1,0:T(1,128)S(1)} %bitcast.7, f32[32,512]{1,0:T(8,128)S(1)} %bitcast.6), custom_call_target="tpu_custom_call" | custom-call | flops 1000000000 | bytes 1000000 | tf_op jit(solution)/shard_map/pallas_call | solution.py:240
  47.9 0.6 %copy.5 = f32[512,32]{0,1:T(8,128)} copy(f32[512,32]{0,1:T(8,128)S(1)} %bitcast.4) | data formatting | bytes 131072
Async XLA Ops:
  0.0 0.7 %copy-start.2 = (s32[32]{0:T(128)S(1)}, s32[32]{0:T(128)}, u32[]{:S(2)}) copy-start(s32[32]{0:T(128)} %param.4) | copy-start | bytes 388
  0.7 0.9 %copy-start = (bf16[512,192]{0,1:T(8,128)(2,1)S(1)}, bf16[512,192]{0,1:T(8,128)(2,1)}, u32[]{:S(2)}) copy-start(bf16[512,192]{0,1:T(8,128)(2,1)} %param.3) | copy-start | bytes 589828
  1.6 0.8 %copy-start.1 = (f32[512,32]{0,1:T(8,128)S(1)}, f32[512,32]{0,1:T(8,128)}, u32[]{:S(2)}) copy-start(f32[512,32]{0,1:T(8,128)} %param.5) | copy-start | bytes 196612

commit v2 on v1

--- a/solution.py
+++ b/solution.py
@@ -41,17 +41,24 @@
     for a in range(nblk):
         unit = (lane == sub + (VECS + 8 * a)).astype(F32)
         blocks.append(jnp.where(lane < VECS, gram[8 * a : 8 * a + 8, :], unit))
-    order = range(VECS - 1, -1, -1) if reverse else range(VECS)
-    for j in order:
-        a, s = divmod(j, 8)
-        pivot = blocks[a][s : s + 1, :]
-        scaled = pivot * (1.0 / pivot[:, j : j + 1])
-        for c in range(nblk):
-            if (c > a and not reverse) or (c < a and reverse):
-                blocks[c] = blocks[c] - blocks[c][:, j : j + 1] * scaled
-            elif c == a:
-                keep = sub < s if reverse else sub > s
-                blocks[c] = blocks[c] - jnp.where(keep, blocks[c][:, j : j + 1], 0.0) * scaled
+    for a in range(nblk - 1, -1, -1) if reverse else range(nblk):
+        others = range(a + 1) if reverse else range(a, nblk)
+        columns = {
+            (c, u): jnp.broadcast_to(blocks[c][:, 8 * a + u : 8 * a + u + 1], (8, 128)) for u in range(8) for c in others
+        }
+        for t in range(7, -1, -1) if reverse else range(8):
+            inner = range(t) if reverse else range(t + 1, 8)
+            keep = sub < t if reverse else sub > t
+            turn = 1.0 / columns[a, t][t : t + 1, :]
+            pivot = blocks[a][t : t + 1, :]
+            tops = {u: columns[a, u][t : t + 1, :] for u in inner}
+            for c in others:
+                factor = columns[c, t] * turn
+                if c == a:
+                    factor = jnp.where(keep, factor, 0.0)
+                for u in inner:
+                    columns[c, u] = columns[c, u] - factor * tops[u]
+                blocks[c] = blocks[c] - factor * pivot
     done = []
     for a in range(nblk):
         diag = jnp.sum(jnp.where(lane == sub + 8 * a, blocks[a], 0.0), axis=1, keepdims=True)
@@ -208,9 +215,7 @@
     u1 = sums1 * inv_row
     y1 = across_lands(u1) * dinv
     sums2 = reduced(4, across_rows(y1 * dinv), z2, r2, t2, a2)
-    gram1 = exact(u1, jnp.concatenate([sums2] * 4, axis=0), NT)
-    back = inverse_factor(gram1, True)
-    y2 = exact(back, across_lands(sums2 * inv_row) * dinv)
+    y2 = across_lands(sums2 * inv_row) * dinv
     gram2 = exact(y2, jnp.concatenate([y2] * 4, axis=0), NT)
     packed = jnp.zeros((8, 128), F32)
     lane8 = lax.broadcasted_iota(jnp.int32, (8, 128), 1)
@@ -219,11 +224,13 @@
     gsrc[...] = packed
     spread(6, lambda to: gsrc, gbuf)
     gbuf[me] = gsrc[...]
+    back = inverse_factor(exact(u1, jnp.concatenate([sums2] * 4, axis=0), NT), True)
     arrived(6, gbuf)
     total = jnp.sum(gbuf[...], axis=0)
     gram2 = jnp.concatenate(
-        [total if a == 0 else pltpu.roll(total, 128 - VECS * a, 1) for a in range(VECS // 8)], axis=0)
-    last = inverse_factor(gram2, False) * math.sqrt(total_rows)
+        [total if a == 0 else pltpu.roll(total, 128 - VECS * a, 1) for a in range(VECS // 8)], axis=0)[:, :VECS]
+    gram2 = exact(exact(back, gram2), jnp.concatenate([back] * 4, axis=0), NT)
+    last = exact(inverse_factor(gram2, False) * math.sqrt(total_rows), back)
     out_ref[...] = exact(last, y2)
     for k, buf in enumerate((lbuf, cbuf, r1, a1, r2, a2, gbuf)):
         left(k, buf)

time: 48.7 us -> 44.4 us (0.912)
  Pallas kernels: 45.4 us -> 41.2 us
    pallas_call x1, Pallas kernels: 45.4 us -> 41.2 us  [local(): pl.pallas_call(functools.partial(body, n, rows * n), out_shape=jax.ShapeD...]
where the time goes in v2:
time: 44.4 us; the launch traced here: 44.2 us
  Pallas kernels  41.2 us (93%)
  local copies, waits for them, and re-layouts  3.05 us (7%)
    pallas_call x1, Pallas kernels, local(): pl.pallas_call(functools.partial(body, n, rows * n), out_shape=jax.ShapeD...  41.2 us
    unnamed x7, local copies, waits for them, and re-layouts  3.05 us

profile of v2, /device:TPU:0, one launch (start us, length us, event | category | flops | bytes accessed | tf_op | source)
XLA Modules:
  0.0 44.2 jit_solution(6093492991514247643)
XLA Ops:
  0.0 0.0 copy-start.2
  0.0 0.7 %copy-done.2 = s32[32]{0:T(128)S(1)} copy-done((s32[32]{0:T(128)S(1)}, s32[32]{0:T(128)}, u32[]{:S(2)}) %copy-start.2) | copy-done | bytes 152
  0.7 0.0 copy-start
  0.7 0.9 %copy-done = bf16[512,192]{0,1:T(8,128)(2,1)S(1)} copy-done((bf16[512,192]{0,1:T(8,128)(2,1)S(1)}, bf16[512,192]{0,1:T(8,128)(2,1)}, u32[]{:S(2)}) %copy-start) | copy-done | bytes 196632
  1.6 0.0 copy-start.1
  1.6 0.8 %copy-done.1 = f32[512,32]{0,1:T(8,128)S(1)} copy-done((f32[512,32]{0,1:T(8,128)S(1)}, f32[512,32]{0,1:T(8,128)}, u32[]{:S(2)}) %copy-start.1) | copy-done | bytes 65560
  2.4 41.2 %shard_map.37 = f32[32,512]{1,0:T(8,128)S(1)} custom-call(bf16[192,512]{1,0:T(8,128)(2,1)S(1)} %bitcast.5, s32[1,32]{1,0:T(1,128)S(1)} %bitcast.7, f32[32,512]{1,0:T(8,128)S(1)} %bitcast.6), custom_call_target="tpu_custom_call" | custom-call | flops 1000000000 | bytes 1000000 | tf_op jit(solution)/shard_map/pallas_call | solution.py:247
  43.6 0.6 %copy.5 = f32[512,32]{0,1:T(8,128)} copy(f32[512,32]{0,1:T(8,128)S(1)} %bitcast.4) | data formatting | bytes 131072
Async XLA Ops:
  0.0 0.7 %copy-start.2 = (s32[32]{0:T(128)S(1)}, s32[32]{0:T(128)}, u32[]{:S(2)}) copy-start(s32[32]{0:T(128)} %param.4) | copy-start | bytes 388
  0.7 0.9 %copy-start = (bf16[512,192]{0,1:T(8,128)(2,1)S(1)}, bf16[512,192]{0,1:T(8,128)(2,1)}, u32[]{:S(2)}) copy-start(bf16[512,192]{0,1:T(8,128)(2,1)} %param.3) | copy-start | bytes 589828
  1.6 0.8 %copy-start.1 = (f32[512,32]{0,1:T(8,128)S(1)}, f32[512,32]{0,1:T(8,128)}, u32[]{:S(2)}) copy-start(f32[512,32]{0,1:T(8,128)} %param.5) | copy-start | bytes 196612

commit v3 on v2

--- a/solution.py
+++ b/solution.py
@@ -225,13 +225,13 @@
     spread(6, lambda to: gsrc, gbuf)
     gbuf[me] = gsrc[...]
     back = inverse_factor(exact(u1, jnp.concatenate([sums2] * 4, axis=0), NT), True)
+    y2 = exact(back, y2) * math.sqrt(total_rows)
     arrived(6, gbuf)
     total = jnp.sum(gbuf[...], axis=0)
     gram2 = jnp.concatenate(
         [total if a == 0 else pltpu.roll(total, 128 - VECS * a, 1) for a in range(VECS // 8)], axis=0)[:, :VECS]
     gram2 = exact(exact(back, gram2), jnp.concatenate([back] * 4, axis=0), NT)
-    last = exact(inverse_factor(gram2, False) * math.sqrt(total_rows), back)
-    out_ref[...] = exact(last, y2)
+    out_ref[...] = exact(inverse_factor(gram2, False), y2)
     for k, buf in enumerate((lbuf, cbuf, r1, a1, r2, a2, gbuf)):
         left(k, buf)
 

time: 44.4 us -> 44.4 us (level)
  no operation moved by 1% of the time
where the time goes in v3:
time: 44.4 us; the launch traced here: 44.2 us
  Pallas kernels  41.1 us (93%)
  local copies, waits for them, and re-layouts  3.05 us (7%)
    pallas_call x1, Pallas kernels, local(): pl.pallas_call(functools.partial(body, n, rows * n), out_shape=jax.ShapeD...  41.1 us
    unnamed x7, local copies, waits for them, and re-layouts  3.05 us

profile of v3, /device:TPU:0, one launch (start us, length us, event | category | flops | bytes accessed | tf_op | source)
XLA Modules:
  0.0 44.2 jit_solution(16813736164486456666)
XLA Ops:
  0.0 0.0 copy-start.2
  0.0 0.7 %copy-done.2 = s32[32]{0:T(128)S(1)} copy-done((s32[32]{0:T(128)S(1)}, s32[32]{0:T(128)}, u32[]{:S(2)}) %copy-start.2) | copy-done | bytes 152
  0.7 0.0 copy-start
  0.7 0.9 %copy-done = bf16[512,192]{0,1:T(8,128)(2,1)S(1)} copy-done((bf16[512,192]{0,1:T(8,128)(2,1)S(1)}, bf16[512,192]{0,1:T(8,128)(2,1)}, u32[]{:S(2)}) %copy-start) | copy-done | bytes 196632
  1.6 0.0 copy-start.1
  1.6 0.8 %copy-done.1 = f32[512,32]{0,1:T(8,128)S(1)} copy-done((f32[512,32]{0,1:T(8,128)S(1)}, f32[512,32]{0,1:T(8,128)}, u32[]{:S(2)}) %copy-start.1) | copy-done | bytes 65560
  2.4 41.1 %shard_map.37 = f32[32,512]{1,0:T(8,128)S(1)} custom-call(bf16[192,512]{1,0:T(8,128)(2,1)S(1)} %bitcast.5, s32[1,32]{1,0:T(1,128)S(1)} %bitcast.7, f32[32,512]{1,0:T(8,128)S(1)} %bitcast.6), custom_call_target="tpu_custom_call" | custom-call | flops 1000000000 | bytes 1000000 | tf_op jit(solution)/shard_map/pallas_call | solution.py:247
  43.5 0.6 %copy.5 = f32[512,32]{0,1:T(8,128)} copy(f32[512,32]{0,1:T(8,128)S(1)} %bitcast.4) | data formatting | bytes 131072
Async XLA Ops:
  0.0 0.7 %copy-start.2 = (s32[32]{0:T(128)S(1)}, s32[32]{0:T(128)}, u32[]{:S(2)}) copy-start(s32[32]{0:T(128)} %param.4) | copy-start | bytes 388
  0.7 0.9 %copy-start = (bf16[512,192]{0,1:T(8,128)(2,1)S(1)}, bf16[512,192]{0,1:T(8,128)(2,1)}, u32[]{:S(2)}) copy-start(bf16[512,192]{0,1:T(8,128)(2,1)} %param.3) | copy-start | bytes 589828
  1.6 0.8 %copy-start.1 = (f32[512,32]{0,1:T(8,128)S(1)}, f32[512,32]{0,1:T(8,128)}, u32[]{:S(2)}) copy-start(f32[512,32]{0,1:T(8,128)} %param.5) | copy-start | bytes 196612
